TPU v7x, 512 devices: a whole 4x8x8 slice. The times are simulated.
512 devices in a mesh: dp: 8 (over x, y_lo), expert: 64 (over y_hi, z, core).
Axes of the slice: x: 4, y: 8 (y_hi: 4, y_lo: 2; y = y_hi * 2 + y_lo), z: 8, core: 2. Of those that a mesh axis runs over, the one named last changes fastest.
Arguments:
- codes: bfloat16 [4096, 7168], P(('dp', 'expert')), may hold values from -6 to 6
- exponents: int32 [4096, 56], P(('dp', 'expert')), may hold values from -2 to 1
- routes: int32 [4096, 8], P(('dp', 'expert')), may hold values from 0 to 63, all different within a row; in each aligned block of 8 rows (0 to 7, 8 to 15, ...) at most 2 rows name the same one
- gate_weight: bfloat16 [64, 7168, 1024], P('expert', None, 'dp'), may hold values from -0.0625 to 0.0625
- up_weight: bfloat16 [64, 7168, 1024], P('expert', None, 'dp'), may hold values from -0.0625 to 0.0625
Outputs:
- hidden: bfloat16 [64, 1024, 1024], P('expert', None, 'dp')
- hessians: float32 [64, 1024, 1024], P('expert', 'dp')
Inputs may be any that keep to these rules, and one draw needn't show every extreme that they name: `routes`: each row names 8 different experts; among the 8 rows of one device no expert is named more than 2 times, and in every draw some expert is named exactly 2 times by the rows of some device.
All inputs are finite; a program needn't handle non-finite values.
Results may differ from a plain program's by a relative error of at most 0.0046.
Values may be sent and summed in bfloat16 or wider, within the bound.
A program may use at most 128 MiB of HBM per device.

v0:
```python
import jax
import jax.numpy as jnp
from jax import lax
from jax.sharding import PartitionSpec as P


def dequantize(codes, exponents):
    scale_full = jnp.zeros(exponents.shape, jnp.float32)
    for exponent_value in range(-2, 2):
        scale_full = scale_full + jnp.where(
            exponents == exponent_value, 2.0**exponent_value, 0.0
        ).astype(jnp.float32)
    block_count = codes.shape[1] // 128
    scaled = (
        codes.reshape(codes.shape[0], block_count, 128)
        * scale_full.astype(jnp.bfloat16)[:, :, None]
    )
    return scaled.reshape(codes.shape)


def slot_matrix(routes, expert_count, capacity):
    chosen = (
        routes[:, :, None] == jnp.arange(expert_count, dtype=jnp.int32)[None, None, :]
    ).astype(jnp.int32)
    counts = jnp.sum(chosen, axis=1)
    earlier = jnp.cumsum(counts, axis=0) - counts
    position = jnp.sum(chosen * earlier[:, None, :], axis=2)
    slot_hot = (
        position[:, :, None] == jnp.arange(capacity, dtype=jnp.int32)[None, None, :]
    ).astype(jnp.float32)
    matrix = jnp.einsum("tke,tkc->ect", chosen.astype(jnp.float32), slot_hot)
    return matrix.astype(jnp.bfloat16)


def shards(codes, exponents, routes, gate_weight, up_weight):
    rows_local = codes.shape[0]
    top_count = routes.shape[1]
    expert_local = gate_weight.shape[0]
    expert_count = lax.axis_size("expert") * expert_local
    groups = lax.axis_size("dp")
    capacity = max(2, (3 * rows_local * top_count + 2 * expert_count - 1) // (2 * expert_count))
    weight_scale = 1.0 / (rows_local * groups * lax.axis_size("expert") * top_count // expert_count)
    gate_local = gate_weight[0]
    up_local = up_weight[0]
    width = codes.shape[1]
    tokens = dequantize(codes, exponents)
    matrix = slot_matrix(routes, expert_count, capacity)
    outgoing = jnp.einsum("ect,td->ecd", matrix, tokens, preferred_element_type=jnp.float32).astype(
        jnp.bfloat16
    )
    arrived = lax.all_to_all(outgoing, "expert", split_axis=0, concat_axis=0, tiled=True)
    arrived = arrived.reshape(-1, width)
    slot_rows = lax.all_gather(arrived, "dp", axis=0, tiled=True)
    gate_part = jnp.dot(slot_rows, gate_local, preferred_element_type=jnp.float32)
    up_part = jnp.dot(slot_rows, up_local, preferred_element_type=jnp.float32)
    hidden = (jax.nn.silu(gate_part) * up_part).astype(jnp.bfloat16)
    moment = lax.dot_general(
        hidden,
        lax.all_gather(hidden, "dp", axis=1, tiled=True),
        (((0,), (0,)), ((), ())),
        preferred_element_type=jnp.float32,
    )
    hessian = moment * weight_scale
    return (hidden[None], hessian[None])


def solution(mesh):
    placed = (
        P(("dp", "expert"), None),
        P(("dp", "expert"), None),
        P(("dp", "expert"), None),
        P("expert", None, "dp"),
        P("expert", None, "dp"),
    )
    return jax.shard_map(
        shards,
        mesh=mesh,
        in_specs=placed,
        out_specs=(P("expert", None, "dp"), P("expert", "dp", None)),
        check_vma=False,
    )
```

profile of v0, /device:TPU:1, one launch (start us, length us, event | category | flops | bytes accessed | tf_op | source)
XLA Modules:
  0.0 453.9 jit_solution(3593832837044066552)
XLA Ops:
  7.2 0.0 copy-start
  7.2 0.0 all-gather.3.cloned.1.call-start
  7.2 0.8 add_convert_fusion
  8.0 0.8 convert_reduce_fusion
  8.9 1.0 select_reduce_fusion
  9.8 0.9 fusion.11
  10.7 0.1 copy.10
  10.8 1.6 convolution_convert_fusion
  12.4 1.9 copy.12
  14.3 64.7 %all_to_all.5 = bf16[64,2,7168]{2,1,0:T(2,128)(2,1)} all-to-all(bf16[64,2,7168]{2,1,0:T(2,128)(2,1)S(1)} %copy.12), channel_id=1, replica_groups=mesh['dp'=8,'expert'=64] {'expert'}, dimensions={0} | all-to-all | bytes 3670016 | tf_op jit(solution)/shard_map/all_to_all | solution.py:51
  79.0 4.9 %reshape.22 = bf16[128,7168]{1,0:T(8,128)(2,1)} reshape(bf16[64,2,7168]{2,1,0:T(2,128)(2,1)} %all_to_all.5) | data formatting | bytes 3670016 | tf_op jit(solution)/shard_map/reshape | solution.py:52
  83.9 0.0 all-gather.3.cloned.1.call-update
  83.9 0.0 all-gather.5.cloned.1.call-start
  84.0 288.7 %all-gather.3.cloned.1.call-done = bf16[1024,7168]{1,0:T(8,128)(2,1)} async-done(((bf16[128,7168]{1,0:T(8,128)(2,1)}), bf16[1024,7168]{1,0:T(8,128)(2,1)}) %all-gather.3.cloned.1.call-update) | async-done | bytes 14680080 | tf_op jit(solution)/shard_map/all_gather | solution.py:53
  372.6 0.0 copy-done
  372.6 0.0 copy-start.1
  372.6 0.0 copy-start.2
  372.6 8.8 %fusion.2 = f32[1024,128]{1,0:T(8,128)S(1)} fusion(bf16[1024,7168]{1,0:T(8,128)(2,1)} %all-gather.3.cloned.1.call-done, bf16[1,7168,128]{2,1,0:T(8,128)(2,1)S(1)} %copy-done), kind=kOutput, calls=%fused_computation.3 | convolution fusion | flops 1879048192 | bytes 17039360 | tf_op jit(solution)/shard_map/dot_general | solution.py:54
  381.4 0.5 copy-done.1
  382.0 0.5 copy-done.2
  382.5 4.6 %fusion.8 = bf16[1024,128]{1,0:T(8,128)(2,1)} fusion(bf16[1024,7168]{1,0:T(8,128)(2,1)S(1)} %copy-done.1, bf16[1,7168,128]{2,1,0:T(8,128)(2,1)S(1)} %copy-done.2, f32[1024,128]{1,0:T(8,128)S(1)} %fusion.2), kind=kOutput, calls=%fused_computation.8 | convolution fusion | flops 1879834624 | bytes 17301504 | tf_op jit(solution)/shard_map/dot_general | solution.py:55
  387.1 0.0 all-gather.5.cloned.1.call-update
  387.2 57.0 %all-gather.5.cloned.1.call-done = bf16[1024,1024]{1,0:T(8,128)(2,1)} async-done(((bf16[1024,128]{1,0:T(8,128)(2,1)}), bf16[1024,1024]{1,0:T(8,128)(2,1)}) %all-gather.5.cloned.1.call-update) | async-done | bytes 2097168 | tf_op jit(solution)/shard_map/all_gather | solution.py:59
  444.1 3.0 fusion.4
  (2 shorter events, 0.0 us)
Async XLA Ops:
  7.2 365.5 %copy-start = (bf16[1,7168,128]{2,1,0:T(8,128)(2,1)S(1)}, bf16[1,7168,128]{2,1,0:T(8,128)(2,1)}, u32[]{:S(2)}) copy-start(bf16[1,7168,128]{2,1,0:T(8,128)(2,1)} %param.8) | copy-start | bytes 5505028
  7.2 365.5 %all-gather.3.cloned.1.call-start = ((), (), s32[]{:S(2)}) async-start(), calls=%async_computation.1 | async-start | bytes 16515072 | tf_op jit(solution)/shard_map/all_gather | solution.py:53
  83.9 360.2 %all-gather.5.cloned.1.call-start = ((), (), s32[]{:S(2)}) async-start(), calls=%async_computation.2 | async-start | bytes 2359296 | tf_op jit(solution)/shard_map/all_gather | solution.py:59
  372.6 9.3 %copy-start.1 = (bf16[1024,7168]{1,0:T(8,128)(2,1)S(1)}, bf16[1024,7168]{1,0:T(8,128)(2,1)}, u32[]{:S(2)}) copy-start(bf16[1024,7168]{1,0:T(8,128)(2,1)} %all-gather.3.cloned.1.call-done) | copy-start | bytes 44040196
  372.6 9.8 %copy-start.2 = (bf16[1,7168,128]{2,1,0:T(8,128)(2,1)S(1)}, bf16[1,7168,128]{2,1,0:T(8,128)(2,1)}, u32[]{:S(2)}) copy-start(bf16[1,7168,128]{2,1,0:T(8,128)(2,1)} %param.9) | copy-start | bytes 5505028
Sparse Core Ops, SparseCore 0:
  84.0 288.5 all-gather.2
  387.3 56.8 all-gather.4
where the time goes:
time: 455 us; the launch traced here: 454 us
  waiting for transfers between devices  346 us (76%)
  blocking collectives  64.7 us (14%)
  matrix products  18.9 us (4%)
  between operations  14.1 us (3%)
  local copies, waits for them, and re-layouts  7.98 us (2%)
    all_gather x1, waiting for transfers between devices, shards(): slot_rows = lax.all_gather(arrived, 'dp', axis=0, tiled=True)  289 us
    all_to_all x1, blocking collectives, shards(): lax.all_to_all(outgoing, 'expert', split_axis=0, concat_axis=0, tiled=True)  64.7 us
    all_gather x1, waiting for transfers between devices, shards(): lax.all_gather(hidden, 'dp', axis=1, tiled=True)  57 us
  transfers between devices with their start and end apart: 2, of which 2 were waited for; matrix products, arithmetic and copies ran while one was open for 0% of the time, Pallas kernels for 0%

commit v1 on v0

v1 whole, which is shorter than its diff:
```python
import functools

import jax
import jax.numpy as jnp
from jax import lax
from jax.experimental import pallas as pl
from jax.experimental.pallas import tpu as pltpu
from jax.sharding import PartitionSpec as P

MESH = pl.DeviceIdType.MESH
F32 = jnp.float32
BF16 = jnp.bfloat16

NX, NY, NZ = 4, 8, 8
TOK = 8
D = 7168
HALF = D // 2
LANES = 128
NC = 4
BLK = HALF // LANES
CB = BLK // NC
KC = CB * LANES
NH = 2
RB = 16
HR = NZ * RB
SL = NX * HR
FB = 128


def kernel(
    scale_out,
    codes,
    exponents,
    routes,
    gate_w,
    up_w,
    hidden_out,
    hess_out,
    deq,
    table,
    deq_in,
    table_in,
    tok,
    sel,
    zsend,
    rows,
    wbuf,
    acc,
    part,
    hall,
    hperm,
    hess,
    core_s,
    core_r,
    y_s,
    y_r,
    z_s,
    z_r,
    x_s,
    x_r,
    w_s,
    w_r,
    p_s,
    p_r,
    hx_s,
    hx_r,
    hc_s,
    hc_r,
    f_s,
    f_r,
):
    dp = lax.axis_index("dp")
    ex = lax.axis_index("expert")
    x, l = dp // 2, dp % 2
    yh, z, c = ex // (2 * NZ), (ex // 2) % NZ, ex % 2
    y = yh * 2 + l
    o = 1 - c
    xr, xl, xo = (x + 1) % NX, (x + 3) % NX, (x + 2) % NX

    def dev(dx, dy, dz, dc):
        return (dx * 2 + dy % 2, ((dy // 2) * NZ + dz) * 2 + dc)

    def remote(src, dst, send, recv, to):
        return pltpu.make_async_remote_copy(
            src_ref=src, dst_ref=dst, send_sem=send, recv_sem=recv, device_id=to, device_id_type=MESH
        )

    other_core = dev(x, y, z, o)
    y_pair = yh * 2 + (1 - l)

    barrier = pltpu.get_barrier_semaphore()

    def greet(to):
        pl.semaphore_signal(barrier, inc=1, device_id=to, device_id_type=MESH)

    def greet_ring(j, carry):
        greet(dev(x, (y + j) % NY, z, c))
        greet(dev(x, y, (z + j) % NZ, c))
        return carry

    greet(other_core)
    greet(dev(x, y_pair, z, o))
    greet(dev(xr, y, z, c))
    greet(dev(xl, y, z, c))
    lax.fori_loop(1, NY, greet_ring, 0)

    ev = exponents[...]
    scale = jnp.zeros(ev.shape, F32)
    for e in range(-2, 2):
        scale = jnp.where(ev == e, jnp.float32(2.0**e), scale)
    for b in range(2 * BLK):
        deq[b] = codes[:, b * LANES : (b + 1) * LANES].astype(F32) * scale[:, b : b + 1]
    rv = routes[...]
    lane = lax.broadcasted_iota(jnp.int32, (TOK, LANES), 1)
    chosen = jnp.zeros((TOK, LANES), F32)
    for t in range(rv.shape[1]):
        chosen = jnp.where(rv[:, t : t + 1] == lane, 1.0, chosen)
    row = lax.broadcasted_iota(jnp.int32, (TOK, LANES), 0)
    order = chosen
    for t in range(TOK - 1):
        order = order + jnp.where(row > t, chosen[t : t + 1, :], 0.0)
    table[...] = chosen * order

    pl.semaphore_wait(barrier, 18)

    def core_copy(n):
        if n == 0:
            return remote(deq.at[pl.ds(o * BLK, BLK)], deq_in, core_s.at[0], core_r.at[0], other_core)
        return remote(table, table_in, core_s.at[1], core_r.at[1], other_core)

    for n in range(2):
        core_copy(n).start()
    for n in range(2):
        core_copy(n).wait_recv()

    def pack(own, oth):
        return jnp.concatenate([jnp.where(c == 0, own, oth), jnp.where(c == 0, oth, own)], axis=0).astype(BF16)

    tok[y, 0] = pack(table[...], table_in[...])

    def assemble(j, carry):
        tok[y, 1 + j] = pack(deq[c * BLK + j], deq_in[j])
        return carry

    lax.fori_loop(0, BLK, assemble, 0)

    def chunk_blocks(k):
        first = 0 if k == 0 else 1 + k * CB
        return pl.ds(first, 1 + (k + 1) * CB - first)

    def y_copy(k, src_y, dst_y):
        part_ref = tok.at[src_y, chunk_blocks(k)]
        return remote(part_ref, part_ref, y_s.at[k, dst_y], y_r.at[k, src_y], dev(x, dst_y, z, c))

    def ring(n, me, act):
        def body(j, carry):
            act((me + j) % n)
            return carry

        lax.fori_loop(1, n, body, 0)

    for k in range(NC):
        ring(NY, y, lambda to, k=k: y_copy(k, y, to).start())

    def w_copy(k, d, m):
        src = (gate_w, up_w)[m].at[pl.ds(d * HALF + k * KC, KC)]
        dst = wbuf.at[k, l * 2 + m]
        return remote(src, dst, w_s.at[k, d, m], w_r.at[k, l * 2 + m], dev(x, yh * 2 + c, z, d))

    def w_local(k, m):
        src = (gate_w, up_w)[m].at[pl.ds(c * HALF + k * KC, KC)]
        return pltpu.make_async_copy(src, wbuf.at[k, l * 2 + m], w_r.at[k, l * 2 + m])

    def w_start(k):
        for m in range(2):
            for d in range(2):
                @pl.when(jnp.logical_or(c != l, c != d))
                def _():
                    w_copy(k, d, m).start()

            @pl.when(c == l)
            def _():
                w_local(k, m).start()

    def w_wait_recv(k):
        for j in range(4):
            pltpu.make_async_copy(wbuf.at[k, j], wbuf.at[k, j], w_r.at[k, j]).wait()

    def w_wait_send(k):
        for m in range(2):
            for d in range(2):
                @pl.when(jnp.logical_or(c != l, c != d))
                def _():
                    w_copy(k, d, m).wait_send()

    def build_selection():
        r = lax.broadcasted_iota(jnp.int32, (NH * HR, LANES), 0)
        q = lax.broadcasted_iota(jnp.int32, (NH * HR, LANES), 1)
        expert = (yh * NZ + (r // RB) % NZ) * 2 + l
        wanted = jnp.where(q == expert, 1.0, 0.0).astype(BF16)
        names = tok[:, 0].reshape(NY * 2 * TOK, LANES)
        place = lax.dot_general(wanted, names, (((1,), (1,)), ((), ())), preferred_element_type=F32)
        r16 = r % RB
        source = ((r // HR) * (NY // NH) + r16 // 4) * 2 + (r16 // 2) % 2
        hit = jnp.logical_and(place == (r16 % 2 + 1).astype(F32), q // TOK == source)
        sel[...] = jnp.where(hit, 1.0, 0.0).astype(BF16).reshape(NH, HR, LANES)

    def z_copy(h, k, src_z, dst_z):
        return remote(
            zsend.at[h, k, dst_z],
            rows.at[h, k, x, src_z],
            z_s.at[h, k, dst_z],
            z_r.at[h, k, src_z],
            dev(x, y, dst_z, c),
        )

    def stage_a(h, k):
        if h == 0:
            ring(NY, y, lambda fr: y_copy(k, fr, fr).wait_recv())
        if h == 0 and k == 0:
            build_selection()
        for j in range(CB):
            names = tok[:, 1 + k * CB + j].reshape(NY * 2 * TOK, LANES)
            got = jnp.dot(sel[h], names, preferred_element_type=F32).astype(BF16)
            zsend[h, k, :, :, j * LANES : (j + 1) * LANES] = got.reshape(NZ, RB, LANES)
        ring(NZ, z, lambda to: z_copy(h, k, z, to).start())
        rows[h, k, x, z] = zsend[h, k, z]

    def x_copy(h, k, n):
        if n == 0:
            ref, to = rows.at[h, k, x], xr
        elif n == 1:
            ref, to = rows.at[h, k, x], xl
        elif n == 2:
            ref, to = rows.at[h, k, xl, pl.ds(0, NZ // 2)], xr
        else:
            ref, to = rows.at[h, k, xr, pl.ds(NZ // 2, NZ // 2)], xl
        return remote(ref, ref, x_s.at[h, k, n], x_r.at[h, k, n], dev(to, y, z, c))

    def x_wait(h, k, n):
        if n == 0:
            ref = rows.at[h, k, xl]
        elif n == 1:
            ref = rows.at[h, k, xr]
        elif n == 2:
            ref = rows.at[h, k, xo, pl.ds(0, NZ // 2)]
        else:
            ref = rows.at[h, k, xo, pl.ds(NZ // 2, NZ // 2)]
        remote(ref, ref, x_s.at[h, k, n], x_r.at[h, k, n], dev(xr, y, z, c)).wait_recv()

    def stage_b(h, k):
        ring(NZ, z, lambda fr: z_copy(h, k, fr, fr).wait_recv())
        x_copy(h, k, 0).start()
        x_copy(h, k, 1).start()

    def stage_c(h, k):
        x_wait(h, k, 0)
        x_copy(h, k, 2).start()
        x_wait(h, k, 1)
        x_copy(h, k, 3).start()

    def stage_d(h, k):
        if h == 0:
            w_wait_recv(k)
        x_wait(h, k, 2)
        x_wait(h, k, 3)

        def body(i, carry):
            left = rows[h, k, pl.ds(2 * i, 2)].reshape(2 * HR, KC)
            for s in range(2):
                right = jnp.concatenate([wbuf[k, 2 * s], wbuf[k, 2 * s + 1]], axis=1)
                got = jnp.dot(left, right, preferred_element_type=F32)
                at = pl.ds(pl.multiple_of(i * 2 * HR, 2 * HR), 2 * HR)
                if k == 0:
                    acc[h, s, at] = got
                else:
                    acc[h, s, at] = acc[h, s, at] + got
            return carry

        lax.fori_loop(0, NX // 2, body, 0)
        if k == NC - 1:
            p_copy(h).start()

    def p_copy(h):
        return remote(acc.at[h, o], part.at[h], p_s.at[h], p_r.at[h], other_core)

    def finish_hidden(h):
        p_copy(h).wait_recv()

        def body(i, carry):
            at = pl.ds(pl.multiple_of(i * HR, HR), HR)
            both = acc[h, c, at] + part[h, at]
            gate, up = both[:, :FB], both[:, FB:]
            value = (gate / (1.0 + jnp.exp(-gate)) * up).astype(BF16)
            hall[h, x, c, at] = value
            return carry

        lax.fori_loop(0, NX, body, 0)
        hx_copy(h, 0).start()
        hx_copy(h, 1).start()
        hc_copy(h, 0).start()

        r = lax.broadcasted_iota(jnp.int32, (HR, HR), 0)
        q = lax.broadcasted_iota(jnp.int32, (HR, HR), 1)
        origin = ((r // 4) % 8) * RB + (((r // 32) % 2) * 2 + r // 64) * 4 + r % 4
        turn = jnp.where(q == origin, 1.0, 0.0).astype(BF16)

        def place(i, carry):
            block = hall[h, x, c, pl.ds(pl.multiple_of(i * HR, HR), HR)]
            got = jnp.dot(turn, block, preferred_element_type=F32).astype(BF16)
            for s in range(2):
                at = pl.multiple_of(i * 2 * HR + s * HR + h * 64, 64)
                hperm[pl.ds(at, 64)] = got[s * 64 : (s + 1) * 64]
            return carry

        lax.fori_loop(0, NX, place, 0)

    def hx_copy(h, n):
        if n == 0:
            ref, to = hall.at[h, x, c], xr
        elif n == 1:
            ref, to = hall.at[h, x, c], xl
        elif n == 2:
            ref, to = hall.at[h, xl, c, pl.ds(0, SL // 2)], xr
        else:
            ref, to = hall.at[h, xr, c, pl.ds(SL // 2, SL // 2)], xl
        return remote(ref, ref, hx_s.at[h, n], hx_r.at[h, n], dev(to, y, z, c))

    def hx_wait(h, n):
        if n == 0:
            ref = hall.at[h, xl, c]
        elif n == 1:
            ref = hall.at[h, xr, c]
        elif n == 2:
            ref = hall.at[h, xo, c, pl.ds(0, SL // 2)]
        else:
            ref = hall.at[h, xo, c, pl.ds(SL // 2, SL // 2)]
        remote(ref, ref, hx_s.at[h, n], hx_r.at[h, n], dev(xr, y, z, c)).wait_recv()

    def hc_copy(h, n):
        ref = hall.at[h, (x, xl, xr, xo)[n], c]
        return remote(ref, ref, hc_s.at[h, n], hc_r.at[h, n], other_core)

    def hc_wait(h, n):
        ref = hall.at[h, (x, xl, xr, xo)[n], o]
        remote(ref, ref, hc_s.at[h, n], hc_r.at[h, n], other_core).wait_recv()

    def relay_hidden(h):
        hx_wait(h, 0)
        hx_copy(h, 2).start()
        hc_copy(h, 1).start()
        hx_wait(h, 1)
        hx_copy(h, 3).start()
        hc_copy(h, 2).start()

    def last_hidden(h):
        hx_wait(h, 2)
        hx_wait(h, 3)
        hc_copy(h, 3).start()

    def hess_part(h, n):
        hc_wait(h, n)
        at = (x, xl, xr, xo)[n]
        right = jnp.concatenate([hall[h, at, 0], hall[h, at, 1]], axis=1)
        got = lax.dot_general(hall[h, x, c], right, (((0,), (0,)), ((), ())), preferred_element_type=F32)
        if h == 0:
            hess[at] = got
        else:
            hess[at] = (hess[at] + got) * scale_out

    steps = [(h, k) for h in range(NH) for k in range(NC)]
    stage_a(*steps[0])
    w_start(0)
    stage_a(*steps[1])
    w_start(1)
    stage_b(*steps[0])
    stage_a(*steps[2])
    w_start(2)
    stage_b(*steps[1])
    stage_c(*steps[0])
    stage_a(*steps[3])
    w_start(3)
    stage_b(*steps[2])
    stage_c(*steps[1])
    stage_a(*steps[4])
    stage_b(*steps[3])
    stage_c(*steps[2])
    stage_d(*steps[0])
    stage_a(*steps[5])
    stage_b(*steps[4])
    stage_c(*steps[3])
    stage_d(*steps[1])
    stage_a(*steps[6])
    stage_b(*steps[5])
    stage_c(*steps[4])
    stage_a(*steps[7])
    stage_d(*steps[2])
    stage_b(*steps[6])
    stage_c(*steps[5])
    stage_d(*steps[3])
    stage_b(*steps[7])
    stage_d(*steps[4])
    stage_c(*steps[6])
    finish_hidden(0)
    stage_d(*steps[5])
    stage_c(*steps[7])
    relay_hidden(0)
    stage_d(*steps[6])
    stage_d(*steps[7])
    last_hidden(0)
    for n in range(4):
        hess_part(0, n)
    finish_hidden(1)
    relay_hidden(1)
    hess_part(1, 0)
    last_hidden(1)

    owner = dev(x, yh * 2 + c, z, l)

    def out_remote(n):
        if n == 0:
            return remote(hperm, hidden_out, f_s.at[0], f_r.at[0], owner)
        return remote(hess.at[n - 1], hess_out.at[n - 1], f_s.at[n], f_r.at[n], owner)

    def out_local(n):
        if n == 0:
            return pltpu.make_async_copy(hperm, hidden_out, f_r.at[0])
        return pltpu.make_async_copy(hess.at[n - 1], hess_out.at[n - 1], f_r.at[n])

    def out_start(n):
        @pl.when(c != l)
        def _():
            out_remote(n).start()

        @pl.when(c == l)
        def _():
            out_local(n).start()

    out_start(0)
    for n in range(1, 4):
        hess_part(1, n)
    for n in range(NX):
        out_start(1 + n)

    for n in range(2):
        core_copy(n).wait_send()
    for k in range(NC):
        ring(NY, y, lambda to, k=k: y_copy(k, y, to).wait_send())
        w_wait_send(k)
    for h, k in steps:
        ring(NZ, z, lambda to, h=h, k=k: z_copy(h, k, z, to).wait_send())
        for n in range(4):
            x_copy(h, k, n).wait_send()
    for h in range(NH):
        p_copy(h).wait_send()
        for n in range(4):
            hx_copy(h, n).wait_send()
            hc_copy(h, n).wait_send()
    for n in range(5):
        @pl.when(c != l)
        def _():
            out_remote(n).wait_send()
        if n == 0:
            pltpu.make_async_copy(hperm, hidden_out, f_r.at[0]).wait()
        else:
            pltpu.make_async_copy(hess.at[n - 1], hess_out.at[n - 1], f_r.at[n]).wait()


def shards(codes, exponents, routes, gate_weight, up_weight):
    sem = pltpu.SemaphoreType.DMA
    vmem = pl.BlockSpec(memory_space=pltpu.VMEM)
    hbm = pl.BlockSpec(memory_space=pl.ANY)
    scale_out = 1.0 / (TOK * NX * NY * NZ * 2 * routes.shape[1] // (NY * NZ))
    hidden, hess = pl.pallas_call(
        functools.partial(kernel, scale_out),
        out_shape=(
            jax.ShapeDtypeStruct((NH * SL, FB), BF16),
            jax.ShapeDtypeStruct((NX, FB, 2 * FB), F32),
        ),
        in_specs=[vmem, vmem, vmem, hbm, hbm],
        out_specs=(hbm, hbm),
        scratch_shapes=[
            pltpu.VMEM((2 * BLK, TOK, LANES), F32),
            pltpu.VMEM((TOK, LANES), F32),
            pltpu.VMEM((BLK, TOK, LANES), F32),
            pltpu.VMEM((TOK, LANES), F32),
            pltpu.VMEM((NY, 1 + BLK, 2 * TOK, LANES), BF16),
            pltpu.VMEM((NH, HR, LANES), BF16),
            pltpu.VMEM((NH, NC, NZ, RB, KC), BF16),
            pltpu.VMEM((NH, NC, NX, NZ, RB, KC), BF16),
            pltpu.VMEM((NC, 4, KC, FB), BF16),
            pltpu.VMEM((NH, 2, SL, 2 * FB), F32),
            pltpu.VMEM((NH, SL, 2 * FB), F32),
            pltpu.VMEM((NH, NX, 2, SL, FB), BF16),
            pltpu.VMEM((NH * SL, FB), BF16),
            pltpu.VMEM((NX, FB, 2 * FB), F32),
            sem((2,)),
            sem((2,)),
            sem((NC, NY)),
            sem((NC, NY)),
            sem((NH, NC, NZ)),
            sem((NH, NC, NZ)),
            sem((NH, NC, 4)),
            sem((NH, NC, 4)),
            sem((NC, 2, 2)),
            sem((NC, 4)),
            sem((NH,)),
            sem((NH,)),
            sem((NH, 4)),
            sem((NH, 4)),
            sem((NH, 4)),
            sem((NH, 4)),
            sem((5,)),
            sem((5,)),
        ],
        compiler_params=pltpu.CompilerParams(
            collective_id=0, has_side_effects=True, vmem_limit_bytes=48 * 1024 * 1024
        ),
        name="routed_stats",
    )(codes, exponents, routes, gate_weight[0], up_weight[0])
    hess = jnp.transpose(hess, (1, 0, 2)).reshape(FB, NX * 2 * FB)
    return hidden[None], hess[None]


def solution(mesh):
    placed = (
        P(("dp", "expert"), None),
        P(("dp", "expert"), None),
        P(("dp", "expert"), None),
        P("expert", None, "dp"),
        P("expert", None, "dp"),
    )
    return jax.shard_map(
        shards,
        mesh=mesh,
        in_specs=placed,
        out_specs=(P("expert", None, "dp"), P("expert", "dp", None)),
        check_vma=False,
    )
```

time: 455 us -> 132 us (0.29)
  waiting for transfers between devices: 346 us -> 0 us
  Pallas kernels: 0 us -> 124 us
  blocking collectives: 64.7 us -> 0 us
  matrix products: 18.9 us -> 0 us
  between operations: 14.1 us -> 0.66 us
    all_gather x2 -> x0, waiting for transfers between devices: 346 us -> none  [the longest x1 289 us: shards(): slot_rows = lax.all_gather(arrived, 'dp', axis=0, tiled=True)]
    pallas_call x0 -> x1, Pallas kernels: none -> 124 us  [shards(): pl.pallas_call(functools.partial(kernel, scale_out), out_shape=(jax.Shape...]
    all_to_all x1 -> x0, blocking collectives: 64.7 us -> none  [shards(): lax.all_to_all(outgoing, 'expert', split_axis=0, concat_axis=0, tiled=True)]
    dot_general x5 -> x0, matrix products: 18.9 us -> none  [the longest x1 8.79 us: shards(): jnp.dot(slot_rows, gate_local, preferred_element_type=jnp.float32)]
    unnamed x6 -> x12, local copies, waits for them, and re-layouts: 1.06 us -> 6.97 us
    reshape x1 -> x0, local copies, waits for them, and re-layouts: 4.93 us -> none  [shards(): arrived = arrived.reshape(-1, width)]
  transfers between devices with their start and end apart: 2 -> 0, of which waited for: 2 -> 0; matrix products, arithmetic and copies ran while one was open for 0% -> 0% of each run, Pallas kernels for 0% -> 0%
where the time goes in v1:
time: 132 us; the launch traced here: 131 us
  Pallas kernels  124 us (94%)
  local copies, waits for them, and re-layouts  7.15 us (5%)
    pallas_call x1, Pallas kernels, shards(): pl.pallas_call(functools.partial(kernel, scale_out), out_shape=(jax.Shape...  124 us
    unnamed x12, local copies, waits for them, and re-layouts  6.97 us

profile of v1, /device:TPU:1, one launch (start us, length us, event | category | flops | bytes accessed | tf_op | source)
XLA Modules:
  0.0 131.3 jit_solution(1638737888790546624)
XLA Ops:
  0.6 0.0 copy-start
  0.6 1.5 %copy-done = bf16[1,7168,128]{2,1,0:T(8,128)(2,1)S(1)} copy-done((bf16[1,7168,128]{2,1,0:T(8,128)(2,1)S(1)}, bf16[1,7168,128]{2,1,0:T(8,128)(2,1)}, u32[]{:S(2)}) %copy-start) | copy-done | bytes 1835032
  2.1 0.0 copy-start.1
  2.1 1.5 %copy-done.1 = bf16[1,7168,128]{2,1,0:T(8,128)(2,1)S(1)} copy-done((bf16[1,7168,128]{2,1,0:T(8,128)(2,1)S(1)}, bf16[1,7168,128]{2,1,0:T(8,128)(2,1)}, u32[]{:S(2)}) %copy-start.1) | copy-done | bytes 1835032
  3.6 0.0 copy-start.2
  3.6 0.9 copy-done.2
  4.5 0.0 copy-start.3
  4.5 0.7 copy-done.3
  5.2 0.0 copy-start.4
  5.2 0.7 copy-done.4
  5.9 123.5 %routed_stats.1 = (bf16[1024,128]{1,0:T(8,128)(2,1)S(1)}, f32[4,128,256]{2,1,0:T(8,128)S(1)}) custom-call(bf16[8,7168]{1,0:T(8,128)(2,1)S(1)} %copy-done.2, s32[8,56]{1,0:T(8,128)S(1)} %copy-done.3, s32[8,8]{1,0:T(8,128)S(1)} %copy-done.4, bf16[7168,128]{1,0:T(8,128)(2,1)S(1)} %bitcast.5, bf16[7168,128]{1,0:T(8,128)(2,1)S(1)} %bitcast.6), custom_call_target="tpu_custom_call" | custom-call | tf_op jit(solution)/shard_map/routed_stats/pallas_call | solution.py:474
  129.4 0.2 copy.7
  129.6 1.0 copy.8
  130.6 0.7 copy.10
Async XLA Ops:
  0.6 1.5 %copy-start = (bf16[1,7168,128]{2,1,0:T(8,128)(2,1)S(1)}, bf16[1,7168,128]{2,1,0:T(8,128)(2,1)}, u32[]{:S(2)}) copy-start(bf16[1,7168,128]{2,1,0:T(8,128)(2,1)} %param.8) | copy-start | bytes 5505028
  2.1 1.5 %copy-start.1 = (bf16[1,7168,128]{2,1,0:T(8,128)(2,1)S(1)}, bf16[1,7168,128]{2,1,0:T(8,128)(2,1)}, u32[]{:S(2)}) copy-start(bf16[1,7168,128]{2,1,0:T(8,128)(2,1)} %param.9) | copy-start | bytes 5505028
  3.6 0.9 copy-start.2
  4.5 0.7 copy-start.3
  5.2 0.7 copy-start.4

commit v2 on v0

v2 whole, which is shorter than its diff:
```python
import functools

import jax
import jax.numpy as jnp
from jax import lax
from jax.experimental import pallas as pl
from jax.experimental.pallas import tpu as pltpu
from jax.sharding import PartitionSpec as P

MESH = pl.DeviceIdType.MESH
F32 = jnp.float32
BF16 = jnp.bfloat16

NX, NY, NZ = 4, 8, 8
TOK = 8
D = 7168
HALF = D // 2
LANES = 128
BLK = HALF // LANES
CUT = 15
NH = 2
RB = 16
CR = NX * NH * RB
SL = NZ * CR
FB = 128
KC = 512
ORDER = (0, 1, 7, 2, 6, 3, 5, 4)
GROUPS = ((0, 4), (4, 6), (6, 8))
PIECES = [(0, 0), (1, 0), (2, 0), (0, 1)] + [(j, 0) for j in range(3, NZ)] + [(j, 1) for j in range(1, NZ)]


def rank_of(distance):
    rank = jnp.zeros_like(distance)
    for j, d in enumerate(ORDER):
        rank = jnp.where(distance == d, j, rank)
    return rank


def kernel(
    scale_out,
    codes_in,
    exponents_in,
    routes_in,
    gate_w,
    up_w,
    hidden_out,
    hess_out,
    codes,
    exponents,
    routes,
    deq,
    table,
    deq_in,
    table_in,
    tok,
    sel,
    zsend,
    rows,
    wbuf,
    acc,
    part,
    hall,
    hown,
    hperm,
    hess,
    in_s,
    core_s,
    core_r,
    y_s,
    y_r,
    z_s,
    z_r,
    x_s,
    x_r,
    w_s,
    w_r,
    p_s,
    p_r,
    hx_s,
    hx_r,
    hc_s,
    hc_r,
    ho_s,
    ho_r,
    f_s,
    f_r,
):
    dp = lax.axis_index("dp")
    ex = lax.axis_index("expert")
    x, l = dp // 2, dp % 2
    yh, z, c = ex // (2 * NZ), (ex // 2) % NZ, ex % 2
    y = yh * 2 + l
    o = 1 - c
    xr, xl, xo = (x + 1) % NX, (x + 3) % NX, (x + 2) % NX
    yr, yl = (y + 1) % NY, (y + NY - 1) % NY

    def dev(dx, dy, dz, dc):
        return (dx * 2 + dy % 2, ((dy // 2) * NZ + dz) * 2 + dc)

    def remote(src, dst, send, recv, to):
        return pltpu.make_async_remote_copy(
            src_ref=src, dst_ref=dst, send_sem=send, recv_sem=recv, device_id=to, device_id_type=MESH
        )

    def ring(n, act):
        def body(j, carry):
            act(j)
            return carry

        lax.fori_loop(1, n, body, 0)

    other_core = dev(x, y, z, o)
    y_pair = yh * 2 + (1 - l)

    inputs = [
        pltpu.make_async_copy(routes_in, routes, in_s.at[0]),
        pltpu.make_async_copy(exponents_in, exponents, in_s.at[1]),
        pltpu.make_async_copy(codes_in, codes, in_s.at[2]),
    ]
    for copy in inputs:
        copy.start()

    barrier = pltpu.get_barrier_semaphore()

    def greet(to):
        pl.semaphore_signal(barrier, inc=1, device_id=to, device_id_type=MESH)

    greet(other_core)
    greet(dev(x, y_pair, z, o))
    greet(dev(x, yr, z, c))
    greet(dev(x, yl, z, c))
    greet(dev(xr, y, z, c))
    greet(dev(xl, y, z, c))
    ring(NZ, lambda j: greet(dev(x, y, (z + j) % NZ, c)))

    inputs[0].wait()
    rv = routes[...]
    lane = lax.broadcasted_iota(jnp.int32, (TOK, LANES), 1)
    chosen = jnp.zeros((TOK, LANES), F32)
    for t in range(rv.shape[1]):
        chosen = jnp.where(rv[:, t : t + 1] == lane, 1.0, chosen)
    row = lax.broadcasted_iota(jnp.int32, (TOK, LANES), 0)
    order = chosen
    for t in range(TOK - 1):
        order = order + jnp.where(row > t, chosen[t : t + 1, :], 0.0)
    table[...] = chosen * order
    inputs[1].wait()
    inputs[2].wait()
    ev = exponents[...]
    scale = jnp.zeros(ev.shape, F32)
    for e in range(-2, 2):
        scale = jnp.where(ev == e, jnp.float32(2.0**e), scale)
    for b in range(2 * BLK):
        deq[b] = codes[:, b * LANES : (b + 1) * LANES].astype(F32) * scale[:, b : b + 1]

    pl.semaphore_wait(barrier, 13)

    def core_copy(n):
        if n == 0:
            return remote(deq.at[pl.ds(o * BLK, BLK)], deq_in, core_s.at[0], core_r.at[0], other_core)
        return remote(table, table_in, core_s.at[1], core_r.at[1], other_core)

    for n in range(2):
        core_copy(n).start()
    for n in range(2):
        core_copy(n).wait_recv()

    def pack(own, oth):
        return jnp.concatenate([jnp.where(c == 0, own, oth), jnp.where(c == 0, oth, own)], axis=0).astype(BF16)

    tok[y, 0] = pack(table[...], table_in[...])

    def assemble(j, carry):
        tok[y, 1 + j] = pack(deq[c * BLK + j], deq_in[j])
        return carry

    lax.fori_loop(0, BLK, assemble, 0, unroll=4)

    def y_ref(src_y, piece):
        return tok.at[src_y, pl.ds(0, CUT) if piece == 0 else pl.ds(CUT, 1 + BLK - CUT)]

    def y_send(step, way, piece):
        src = (y + NY - step) % NY if way == 0 else (y + step) % NY
        to = yr if way == 0 else yl
        ref = y_ref(src, piece)
        return remote(ref, ref, y_s.at[step, way, piece], y_r.at[step, way, piece], dev(x, to, z, c))

    def y_wait(step, way, piece):
        src = (y + NY - step - 1) % NY if way == 0 else (y + step + 1) % NY
        ref = y_ref(src, piece)
        remote(ref, ref, y_s.at[step, way, piece], y_r.at[step, way, piece], dev(x, yr, z, c)).wait_recv()

    y_all = [(step, way, piece) for step in range(4) for piece in range(2) for way in range(2) if step < 3 or way == piece]

    def y_hop(step):
        for s, way, piece in y_all:
            if s == step:
                y_wait(s, way, piece)
                if (s + 1, way, piece) in y_all:
                    y_send(s + 1, way, piece).start()

    def w_copy(d, m):
        src = (gate_w, up_w)[m].at[pl.ds(d * HALF, HALF)]
        return remote(src, wbuf.at[l * 2 + m], w_s.at[d, m], w_r.at[l * 2 + m], dev(x, yh * 2 + c, z, d))

    def w_local(m):
        src = (gate_w, up_w)[m].at[pl.ds(c * HALF, HALF)]
        return pltpu.make_async_copy(src, wbuf.at[l * 2 + m], w_r.at[l * 2 + m])

    def w_start():
        for m in range(2):
            for d in range(2):
                @pl.when(jnp.logical_or(c != l, c != d))
                def _():
                    w_copy(d, m).start()

            @pl.when(c == l)
            def _():
                w_local(m).start()

    def w_wait_recv():
        for j in range(4):
            pltpu.make_async_copy(wbuf.at[j], wbuf.at[j], w_r.at[j]).wait()

    def w_wait_send():
        for m in range(2):
            for d in range(2):
                @pl.when(jnp.logical_or(c != l, c != d))
                def _():
                    w_copy(d, m).wait_send()

    def near(h, b):
        return jnp.concatenate([tok[(y + d) % NY, b] for d in ORDER[h * 4 : h * 4 + 4]], axis=0)

    def select(h):
        r = lax.broadcasted_iota(jnp.int32, (NZ * RB, LANES), 0)
        q = lax.broadcasted_iota(jnp.int32, (NZ * RB, LANES), 1)
        wanted = jnp.where(q == (yh * NZ + r // RB) * 2 + l, 1.0, 0.0).astype(BF16)
        place = lax.dot_general(wanted, near(h, 0), (((1,), (1,)), ((), ())), preferred_element_type=F32)
        r = lax.broadcasted_iota(jnp.int32, place.shape, 0)
        q = lax.broadcasted_iota(jnp.int32, place.shape, 1)
        hit = jnp.logical_and(place == (r % 2 + 1).astype(F32), q // TOK == (r % RB) // 2)
        sel[...] = jnp.where(hit, 1.0, 0.0).astype(BF16)
        for b in range(0, BLK, 2):
            names = jnp.concatenate([near(h, 1 + b), near(h, 2 + b)], axis=1)
            got = jnp.dot(sel[...], names, preferred_element_type=F32).astype(BF16)
            zsend[h, :, :, b * LANES : (b + 2) * LANES] = got.reshape(NZ, RB, 2 * LANES)
        rows[x, 0, h] = zsend[h, z]

    def z_copy(h, j):
        d = ORDER[j]
        to = (z + NZ - d) % NZ
        return remote(zsend.at[h, to], rows.at[x, j, h], z_s.at[h, j], z_r.at[h, j], dev(x, y, to, c))

    def z_start(h):
        for j in range(1, NZ):
            z_copy(h, j).start()

    def x_refs(i, n, mine):
        j, h = PIECES[i]
        if n < 2:
            return rows.at[(x if mine else (xl, xr)[n]), j, h]
        at = (xl, xr)[n - 2] if mine else xo
        return rows.at[at, j, h, :, pl.ds((n - 2) * (HALF // 2), HALF // 2)]

    def x_copy(i, n):
        ref = x_refs(i, n, True)
        return remote(ref, ref, x_s.at[i, n], x_r.at[i, n], dev((xr, xl)[n % 2], y, z, c))

    def x_wait(i, n):
        ref = x_refs(i, n, False)
        remote(ref, ref, x_s.at[i, n], x_r.at[i, n], dev(xr, y, z, c)).wait_recv()

    def stage_b(i):
        j, h = PIECES[i]
        if j > 0:
            z_copy(h, j).wait_recv()
        x_copy(i, 0).start()
        x_copy(i, 1).start()

    def stage_c(i):
        for n in range(2):
            x_wait(i, n)
            x_copy(i, 2 + n).start()

    def stage_d(j):
        if j == 0:
            w_wait_recv()
        for h in range(NH):
            i = PIECES.index((j, h))
            x_wait(i, 2)
            x_wait(i, 3)
        for s in range(2):
            got = None
            for k in range(HALF // KC):
                cols = pl.ds(k * KC, KC)
                left = rows[:, j, :, :, cols].reshape(CR, KC)
                right = jnp.concatenate([wbuf[2 * s, cols], wbuf[2 * s + 1, cols]], axis=1)
                term = jnp.dot(left, right, preferred_element_type=F32)
                got = term if got is None else got + term
            acc[s, pl.ds(j * CR, CR)] = got

    def group_rows(g):
        first, last = GROUPS[g]
        return pl.ds(first * CR, (last - first) * CR)

    def p_copy(g):
        at = group_rows(g)
        return remote(acc.at[o, at], part.at[at], p_s.at[g], p_r.at[g], other_core)

    owner = dev(x, yh * 2 + c, z, l)

    def ho_remote(g):
        at = group_rows(g)
        return remote(hall.at[x, c, at], hown.at[at], ho_s.at[g], ho_r.at[g], owner)

    def ho_local(g):
        at = group_rows(g)
        return pltpu.make_async_copy(hall.at[x, c, at], hown.at[at], ho_r.at[g])

    def finish_hidden(g):
        p_copy(g).wait_recv()
        first, last = GROUPS[g]

        def body(j, carry):
            at = pl.ds(pl.multiple_of(j * CR, CR), CR)
            both = acc[c, at] + part[at]
            gate, up = both[:, :FB], both[:, FB:]
            hall[x, c, at] = (gate / (1.0 + jnp.exp(-gate)) * up).astype(BF16)
            return carry

        lax.fori_loop(first, last, body, 0)
        hx_copy(g, 0).start()
        hx_copy(g, 1).start()
        hc_copy(g, 0).start()

        @pl.when(c != l)
        def _():
            ho_remote(g).start()

        @pl.when(c == l)
        def _():
            ho_local(g).start()

    def hx_refs(g, n, mine):
        first, last = GROUPS[g]
        size = (last - first) * CR
        if n < 2:
            return hall.at[(x if mine else (xl, xr)[n]), c, pl.ds(first * CR, size)]
        at = (xl, xr)[n - 2] if mine else xo
        return hall.at[at, c, pl.ds(first * CR + (n - 2) * (size // 2), size // 2)]

    def hx_copy(g, n):
        ref = hx_refs(g, n, True)
        return remote(ref, ref, hx_s.at[g, n], hx_r.at[g, n], dev((xr, xl)[n % 2], y, z, c))

    def hx_wait(g, n):
        ref = hx_refs(g, n, False)
        remote(ref, ref, hx_s.at[g, n], hx_r.at[g, n], dev(xr, y, z, c)).wait_recv()

    def hc_copy(g, n):
        ref = hall.at[(x, xl, xr, xo)[n], c, group_rows(g)]
        return remote(ref, ref, hc_s.at[g, n], hc_r.at[g, n], other_core)

    def hc_wait(g, n):
        ref = hall.at[(x, xl, xr, xo)[n], o, group_rows(g)]
        remote(ref, ref, hc_s.at[g, n], hc_r.at[g, n], other_core).wait_recv()

    def relay_hidden(g):
        for n in range(2):
            hx_wait(g, n)
            hx_copy(g, 2 + n).start()
            hc_copy(g, 1 + n).start()

    def last_hidden(g):
        hx_wait(g, 2)
        hx_wait(g, 3)
        hc_copy(g, 3).start()

    def hess_cols(n):
        at = (x, xl, xr, xo)[n]
        return pl.ds(pl.multiple_of(at * 2 * FB, 2 * FB), 2 * FB)

    def hess_part(g, n):
        hc_wait(g, n)
        at = (x, xl, xr, xo)[n]
        r = group_rows(g)
        right = jnp.concatenate([hall[at, 0, r], hall[at, 1, r]], axis=1)
        got = lax.dot_general(hall[x, c, r], right, (((0,), (0,)), ((), ())), preferred_element_type=F32)
        cols = hess_cols(n)
        if g == 0:
            hess[:, cols] = got
        elif g < len(GROUPS) - 1:
            hess[:, cols] = hess[:, cols] + got
        else:
            hess[:, cols] = (hess[:, cols] + got) * scale_out

    def out_remote(n):
        cols = hess_cols(n)
        return remote(hess.at[:, cols], hess_out.at[:, cols], f_s.at[n], f_r.at[n], owner)

    def out_local(n):
        cols = hess_cols(n)
        return pltpu.make_async_copy(hess.at[:, cols], hess_out.at[:, cols], f_r.at[n])

    def out_start(n):
        @pl.when(c != l)
        def _():
            out_remote(n).start()

        @pl.when(c == l)
        def _():
            out_local(n).start()

    def restore():
        for g in range(len(GROUPS)):
            ho_local(g).wait()
        r = lax.broadcasted_iota(jnp.int32, (NZ * NH * RB, NZ * NH * RB), 0)
        q = lax.broadcasted_iota(jnp.int32, (NZ * NH * RB, NZ * NH * RB), 1)
        y_at = ((r // 32) % 4) * 2 + r // 128
        y_rank = rank_of((y_at + NY - (yh * 2 + c)) % NY)
        z_rank = rank_of(((r // 4) % NZ + NZ - z) % NZ)
        turn = jnp.where(q == z_rank * (NH * RB) + y_rank * 4 + r % 4, 1.0, 0.0).astype(BF16)
        for s in range(NX):
            block = jnp.concatenate([hown[j * CR + s * NH * RB : j * CR + (s + 1) * NH * RB] for j in range(NZ)], axis=0)
            hperm[s * 256 : (s + 1) * 256] = jnp.dot(turn, block, preferred_element_type=F32).astype(BF16)

    for piece in range(2):
        for way in range(2):
            y_send(0, way, piece).start()
    y_hop(0)
    y_hop(1)
    select(0)
    stage_b(0)
    z_start(0)
    y_hop(2)
    w_start()
    y_hop(3)
    select(1)
    z_start(1)
    stage_b(1)
    stage_c(0)
    stage_b(2)
    stage_b(3)
    stage_c(1)
    for i in range(4, 12):
        stage_b(i)
        stage_c(i - 2)
    stage_b(12)
    stage_c(10)
    stage_d(0)
    stage_d(1)
    stage_b(13)
    stage_c(11)
    stage_d(2)
    stage_b(14)
    stage_c(12)
    stage_d(3)
    p_copy(0).start()
    stage_b(15)
    stage_c(13)
    stage_d(4)
    finish_hidden(0)
    stage_c(14)
    stage_d(5)
    p_copy(1).start()
    stage_c(15)
    relay_hidden(0)
    finish_hidden(1)
    stage_d(6)
    stage_d(7)
    p_copy(2).start()
    last_hidden(0)
    relay_hidden(1)
    for n in range(4):
        hess_part(0, n)
    finish_hidden(2)
    last_hidden(1)
    for n in range(4):
        hess_part(1, n)
    hess_part(2, 0)
    out_start(0)
    relay_hidden(2)
    for n in (1, 2):
        hess_part(2, n)
        out_start(n)
    last_hidden(2)
    hess_part(2, 3)
    out_start(3)
    restore()
    hidden_copy = pltpu.make_async_copy(hperm, hidden_out, in_s.at[0])
    hidden_copy.start()

    for n in range(2):
        core_copy(n).wait_send()
    for step, way, piece in y_all:
        y_send(step, way, piece).wait_send()
    w_wait_send()
    for h in range(NH):
        for j in range(1, NZ):
            z_copy(h, j).wait_send()
    for i in range(len(PIECES)):
        for n in range(4):
            x_copy(i, n).wait_send()
    for g in range(len(GROUPS)):
        p_copy(g).wait_send()
        for n in range(4):
            hx_copy(g, n).wait_send()
            hc_copy(g, n).wait_send()

        @pl.when(c != l)
        def _():
            ho_remote(g).wait_send()

    for n in range(4):
        @pl.when(c != l)
        def _():
            out_remote(n).wait_send()

        out_local(n).wait()
    hidden_copy.wait()


def shards(codes, exponents, routes, gate_weight, up_weight):
    sem = pltpu.SemaphoreType.DMA
    hbm = pl.BlockSpec(memory_space=pl.ANY)
    scale_out = 1.0 / (TOK * NX * NY * NZ * 2 * routes.shape[1] // (NY * NZ))
    groups = len(GROUPS)
    hidden, hess = pl.pallas_call(
        functools.partial(kernel, scale_out),
        out_shape=(
            jax.ShapeDtypeStruct((SL, FB), BF16),
            jax.ShapeDtypeStruct((FB, NX * 2 * FB), F32),
        ),
        in_specs=[hbm] * 5,
        out_specs=(hbm, hbm),
        scratch_shapes=[
            pltpu.VMEM(codes.shape, BF16),
            pltpu.VMEM(exponents.shape, jnp.int32),
            pltpu.VMEM(routes.shape, jnp.int32),
            pltpu.VMEM((2 * BLK, TOK, LANES), F32),
            pltpu.VMEM((TOK, LANES), F32),
            pltpu.VMEM((BLK, TOK, LANES), F32),
            pltpu.VMEM((TOK, LANES), F32),
            pltpu.VMEM((NY, 1 + BLK, 2 * TOK, LANES), BF16),
            pltpu.VMEM((NZ * RB, 8 * TOK), BF16),
            pltpu.VMEM((NH, NZ, RB, HALF), BF16),
            pltpu.VMEM((NX, NZ, NH, RB, HALF), BF16),
            pltpu.VMEM((4, HALF, FB), BF16),
            pltpu.VMEM((2, SL, 2 * FB), F32),
            pltpu.VMEM((SL, 2 * FB), F32),
            pltpu.VMEM((NX, 2, SL, FB), BF16),
            pltpu.VMEM((SL, FB), BF16),
            pltpu.VMEM((SL, FB), BF16),
            pltpu.VMEM((FB, NX * 2 * FB), F32),
            sem((3,)),
            sem((2,)),
            sem((2,)),
            sem((4, 2, 2)),
            sem((4, 2, 2)),
            sem((NH, NZ)),
            sem((NH, NZ)),
            sem((len(PIECES), 4)),
            sem((len(PIECES), 4)),
            sem((2, 2)),
            sem((4,)),
            sem((groups,)),
            sem((groups,)),
            sem((groups, 4)),
            sem((groups, 4)),
            sem((groups, 4)),
            sem((groups, 4)),
            sem((groups,)),
            sem((groups,)),
            sem((4,)),
            sem((4,)),
        ],
        compiler_params=pltpu.CompilerParams(
            collective_id=0, has_side_effects=True, vmem_limit_bytes=60 * 1024 * 1024
        ),
        name="routed_stats",
    )(codes, exponents, routes, gate_weight[0], up_weight[0])
    return hidden[None], hess[None]


def solution(mesh):
    placed = (
        P(("dp", "expert"), None),
        P(("dp", "expert"), None),
        P(("dp", "expert"), None),
        P("expert", None, "dp"),
        P("expert", None, "dp"),
    )
    return jax.shard_map(
        shards,
        mesh=mesh,
        in_specs=placed,
        out_specs=(P("expert", None, "dp"), P("expert", "dp", None)),
        check_vma=False,
    )
```

time: 455 us -> 115 us (0.25)
  waiting for transfers between devices: 346 us -> 0 us
  Pallas kernels: 0 us -> 111 us
  blocking collectives: 64.7 us -> 0 us
  matrix products: 18.9 us -> 0 us
  between operations: 14.1 us -> 0.64 us
    all_gather x2 -> x0, waiting for transfers between devices: 346 us -> none  [the longest x1 289 us: shards(): slot_rows = lax.all_gather(arrived, 'dp', axis=0, tiled=True)]
    pallas_call x0 -> x1, Pallas kernels: none -> 111 us  [shards(): pl.pallas_call(functools.partial(kernel, scale_out), out_shape=(jax.Shape...]
    all_to_all x1 -> x0, blocking collectives: 64.7 us -> none  [shards(): lax.all_to_all(outgoing, 'expert', split_axis=0, concat_axis=0, tiled=True)]
    dot_general x5 -> x0, matrix products: 18.9 us -> none  [the longest x1 8.79 us: shards(): jnp.dot(slot_rows, gate_local, preferred_element_type=jnp.float32)]
    reshape x1 -> x0, local copies, waits for them, and re-layouts: 4.93 us -> none  [shards(): arrived = arrived.reshape(-1, width)]
  transfers between devices with their start and end apart: 2 -> 0, of which waited for: 2 -> 0; matrix products, arithmetic and copies ran while one was open for 0% -> 0% of each run, Pallas kernels for 0% -> 0%
where the time goes in v2:
time: 115 us
  Pallas kernels  111 us (97%)
  local copies, waits for them, and re-layouts  3.55 us (3%)
    pallas_call x1, Pallas kernels, shards(): pl.pallas_call(functools.partial(kernel, scale_out), out_shape=(jax.Shape...  111 us
    unnamed x2, local copies, waits for them, and re-layouts  3.55 us

profile of v2, /device:TPU:1, one launch (start us, length us, event | category | flops | bytes accessed | tf_op | source)
XLA Modules:
  0.0 114.9 jit_solution(5217142209500105074)
XLA Ops:
  0.6 110.7 %routed_stats.1 = (bf16[1024,128]{1,0:T(8,128)(2,1)}, f32[128,1024]{1,0:T(8,128)}) custom-call(bf16[8,7168]{1,0:T(8,128)(2,1)} %codes_in.1, s32[8,56]{1,0:T(8,128)} %exponents_in.1, s32[8,8]{1,0:T(8,128)} %routes_in.1, bf16[7168,128]{1,0:T(8,128)(2,1)} %bitcast.4, bf16[7168,128]{1,0:T(8,128)(2,1)} %bitcast.5), custom_call_target="tpu_custom_call" | custom-call | tf_op jit(solution)/shard_map/routed_stats/pallas_call | solution.py:529
  111.4 1.7 %copy.9 = bf16[1,1024,128]{2,1,0:T(8,128)(2,1)} copy(bf16[1,1024,128]{2,1,0:T(8,128)(2,1)} %bitcast.7) | data formatting | bytes 524288
  113.0 1.9 %copy.10 = f32[1,128,1024]{2,1,0:T(8,128)} copy(f32[1,128,1024]{2,1,0:T(8,128)} %bitcast.6) | data formatting | bytes 1048576

commit v3 on v2

--- a/solution.py
+++ b/solution.py
@@ -25,8 +25,16 @@
 FB = 128
 KC = 512
 ORDER = (0, 1, 7, 2, 6, 3, 5, 4)
-GROUPS = ((0, 4), (4, 6), (6, 8))
-PIECES = [(0, 0), (1, 0), (2, 0), (0, 1)] + [(j, 0) for j in range(3, NZ)] + [(j, 1) for j in range(1, NZ)]
+GROUPS = ((0, 4), (4, 8))
+PIECES = [(0, 0), (1, 0), (2, 0), (0, 1), (1, 1), (2, 1), (3, 0), (4, 0), (3, 1), (4, 1)]
+PIECES += [(5, 0), (6, 0), (5, 1), (6, 1), (7, 0), (7, 1)]
+AHEAD = 4
+PLAN = (
+    "B3", "C1", "B4", "C2", "B5", "C3", "B6", "C4", "B7", "C5", "B8", "C6", "B9", "C7", "B10", "C8",
+    "B11", "C9", "B12", "C10", "B13", "C11", "B14", "C12", "B15", "D0", "D1", "C13", "D2", "D3", "P0", "C14",
+    "D4", "C15", "F0", "D5", "D6", "D7", "P1", "R0", "F1", "L0", "R1", "H0", "E0", "E1", "E2", "L1",
+    "E3",
+)
 
 
 def rank_of(distance):
@@ -252,9 +260,11 @@
         to = (z + NZ - d) % NZ
         return remote(zsend.at[h, to], rows.at[x, j, h], z_s.at[h, j], z_r.at[h, j], dev(x, y, to, c))
 
-    def z_start(h):
-        for j in range(1, NZ):
-            z_copy(h, j).start()
+    z_order = [(h, j) for j, h in PIECES if j > 0]
+
+    def z_start(n):
+        if n < len(z_order):
+            z_copy(*z_order[n]).start()
 
     def x_refs(i, n, mine):
         j, h = PIECES[i]
@@ -275,6 +285,7 @@
         j, h = PIECES[i]
         if j > 0:
             z_copy(h, j).wait_recv()
+            z_start(z_order.index((h, j)) + AHEAD)
         x_copy(i, 0).start()
         x_copy(i, 1).start()
 
@@ -388,12 +399,9 @@
         right = jnp.concatenate([hall[at, 0, r], hall[at, 1, r]], axis=1)
         got = lax.dot_general(hall[x, c, r], right, (((0,), (0,)), ((), ())), preferred_element_type=F32)
         cols = hess_cols(n)
-        if g == 0:
-            hess[:, cols] = got
-        elif g < len(GROUPS) - 1:
-            hess[:, cols] = hess[:, cols] + got
-        else:
-            hess[:, cols] = (hess[:, cols] + got) * scale_out
+        if g > 0:
+            got = hess[:, cols] + got
+        hess[:, cols] = got * scale_out if g == len(GROUPS) - 1 else got
 
     def out_remote(n):
         cols = hess_cols(n)
@@ -433,60 +441,29 @@
     select(0)
     stage_b(0)
     z_start(0)
+    z_start(1)
     y_hop(2)
     w_start()
+    stage_b(1)
+    stage_c(0)
     y_hop(3)
     select(1)
-    z_start(1)
-    stage_b(1)
-    stage_c(0)
+    for n in range(2, AHEAD):
+        z_start(n)
     stage_b(2)
-    stage_b(3)
-    stage_c(1)
-    for i in range(4, 12):
-        stage_b(i)
-        stage_c(i - 2)
-    stage_b(12)
-    stage_c(10)
-    stage_d(0)
-    stage_d(1)
-    stage_b(13)
-    stage_c(11)
-    stage_d(2)
-    stage_b(14)
-    stage_c(12)
-    stage_d(3)
-    p_copy(0).start()
-    stage_b(15)
-    stage_c(13)
-    stage_d(4)
-    finish_hidden(0)
-    stage_c(14)
-    stage_d(5)
-    p_copy(1).start()
-    stage_c(15)
-    relay_hidden(0)
-    finish_hidden(1)
-    stage_d(6)
-    stage_d(7)
-    p_copy(2).start()
-    last_hidden(0)
-    relay_hidden(1)
-    for n in range(4):
-        hess_part(0, n)
-    finish_hidden(2)
-    last_hidden(1)
-    for n in range(4):
-        hess_part(1, n)
-    hess_part(2, 0)
-    out_start(0)
-    relay_hidden(2)
-    for n in (1, 2):
-        hess_part(2, n)
-        out_start(n)
-    last_hidden(2)
-    hess_part(2, 3)
-    out_start(3)
+    acts = {"B": stage_b, "C": stage_c, "D": stage_d, "F": finish_hidden, "R": relay_hidden, "L": last_hidden}
+    for step in PLAN:
+        act, n = step[0], int(step[1:])
+        if act == "P":
+            p_copy(n).start()
+        elif act == "H":
+            for m in range(4):
+                hess_part(n, m)
+        elif act == "E":
+            hess_part(len(GROUPS) - 1, n)
+            out_start(n)
+        else:
+            acts[act](n)
     restore()
     hidden_copy = pltpu.make_async_copy(hperm, hidden_out, in_s.at[0])
     hidden_copy.start()

time: 115 us -> 112 us (0.974)
  Pallas kernels: 111 us -> 107 us
    pallas_call x1, Pallas kernels: 111 us -> 107 us  [shards(): pl.pallas_call(functools.partial(kernel, scale_out), out_shape=(jax.Shape...]
where the time goes in v3:
time: 112 us
  Pallas kernels  107 us (96%)
  local copies, waits for them, and re-layouts  3.55 us (3%)
    pallas_call x1, Pallas kernels, shards(): pl.pallas_call(functools.partial(kernel, scale_out), out_shape=(jax.Shape...  107 us
    unnamed x2, local copies, waits for them, and re-layouts  3.55 us

profile of v3, /device:TPU:1, one launch (start us, length us, event | category | flops | bytes accessed | tf_op | source)
XLA Modules:
  0.0 111.6 jit_solution(16463557632259997645)
XLA Ops:
  0.6 107.4 %routed_stats.1 = (bf16[1024,128]{1,0:T(8,128)(2,1)}, f32[128,1024]{1,0:T(8,128)}) custom-call(bf16[8,7168]{1,0:T(8,128)(2,1)} %codes_in.1, s32[8,56]{1,0:T(8,128)} %exponents_in.1, s32[8,8]{1,0:T(8,128)} %routes_in.1, bf16[7168,128]{1,0:T(8,128)(2,1)} %bitcast.4, bf16[7168,128]{1,0:T(8,128)(2,1)} %bitcast.5), custom_call_target="tpu_custom_call" | custom-call | tf_op jit(solution)/shard_map/routed_stats/pallas_call | solution.py:506
  108.0 1.7 %copy.9 = bf16[1,1024,128]{2,1,0:T(8,128)(2,1)} copy(bf16[1,1024,128]{2,1,0:T(8,128)(2,1)} %bitcast.7) | data formatting | bytes 524288
  109.7 1.9 %copy.10 = f32[1,128,1024]{2,1,0:T(8,128)} copy(f32[1,128,1024]{2,1,0:T(8,128)} %bitcast.6) | data formatting | bytes 1048576

commit v4 on v3

--- a/solution.py
+++ b/solution.py
@@ -31,9 +31,8 @@
 AHEAD = 4
 PLAN = (
     "B3", "C1", "B4", "C2", "B5", "C3", "B6", "C4", "B7", "C5", "B8", "C6", "B9", "C7", "B10", "C8",
-    "B11", "C9", "B12", "C10", "B13", "C11", "B14", "C12", "B15", "D0", "D1", "C13", "D2", "D3", "P0", "C14",
-    "D4", "C15", "F0", "D5", "D6", "D7", "P1", "R0", "F1", "L0", "R1", "H0", "E0", "E1", "E2", "L1",
-    "E3",
+    "B11", "C9", "B12", "C10", "B13", "C11", "B14", "C12", "B15", "C13", "D0", "D1", "C14", "D2", "D3", "C15",
+    "D4", "F0", "D5", "D6", "D7", "R0", "F1", "L0", "R1", "H0", "E0", "E1", "E2", "L1", "E3",
 )
 
 
@@ -249,11 +248,19 @@
         q = lax.broadcasted_iota(jnp.int32, place.shape, 1)
         hit = jnp.logical_and(place == (r % 2 + 1).astype(F32), q // TOK == (r % RB) // 2)
         sel[...] = jnp.where(hit, 1.0, 0.0).astype(BF16)
+
+    def fill(h, first, last):
+        to = [(z + NZ - d) % NZ for d in ORDER[first:last]]
+        chosen = jnp.concatenate([sel[pl.ds(pl.multiple_of(t * RB, RB), RB)] for t in to], axis=0)
         for b in range(0, BLK, 2):
             names = jnp.concatenate([near(h, 1 + b), near(h, 2 + b)], axis=1)
-            got = jnp.dot(sel[...], names, preferred_element_type=F32).astype(BF16)
-            zsend[h, :, :, b * LANES : (b + 2) * LANES] = got.reshape(NZ, RB, 2 * LANES)
-        rows[x, 0, h] = zsend[h, z]
+            got = jnp.dot(chosen, names, preferred_element_type=F32).astype(BF16)
+            for n, t in enumerate(to):
+                piece = got[n * RB : (n + 1) * RB]
+                if first + n == 0:
+                    rows[x, 0, h, :, b * LANES : (b + 2) * LANES] = piece
+                else:
+                    zsend[h, t, :, b * LANES : (b + 2) * LANES] = piece
 
     def z_copy(h, j):
         d = ORDER[j]
@@ -310,14 +317,15 @@
                 term = jnp.dot(left, right, preferred_element_type=F32)
                 got = term if got is None else got + term
             acc[s, pl.ds(j * CR, CR)] = got
+        p_copy(j).start()
 
     def group_rows(g):
         first, last = GROUPS[g]
         return pl.ds(first * CR, (last - first) * CR)
 
-    def p_copy(g):
-        at = group_rows(g)
-        return remote(acc.at[o, at], part.at[at], p_s.at[g], p_r.at[g], other_core)
+    def p_copy(j):
+        at = pl.ds(j * CR, CR)
+        return remote(acc.at[o, at], part.at[at], p_s.at[j], p_r.at[j], other_core)
 
     owner = dev(x, yh * 2 + c, z, l)
 
@@ -330,17 +338,12 @@
         return pltpu.make_async_copy(hall.at[x, c, at], hown.at[at], ho_r.at[g])
 
     def finish_hidden(g):
-        p_copy(g).wait_recv()
-        first, last = GROUPS[g]
-
-        def body(j, carry):
-            at = pl.ds(pl.multiple_of(j * CR, CR), CR)
+        for j in range(*GROUPS[g]):
+            p_copy(j).wait_recv()
+            at = pl.ds(j * CR, CR)
             both = acc[c, at] + part[at]
             gate, up = both[:, :FB], both[:, FB:]
             hall[x, c, at] = (gate / (1.0 + jnp.exp(-gate)) * up).astype(BF16)
-            return carry
-
-        lax.fori_loop(first, last, body, 0)
         hx_copy(g, 0).start()
         hx_copy(g, 1).start()
         hc_copy(g, 0).start()
@@ -439,24 +442,25 @@
     y_hop(0)
     y_hop(1)
     select(0)
+    fill(0, 0, 3)
     stage_b(0)
     z_start(0)
     z_start(1)
     y_hop(2)
+    fill(0, 3, NZ)
     w_start()
     stage_b(1)
     stage_c(0)
     y_hop(3)
     select(1)
+    fill(1, 0, NZ)
     for n in range(2, AHEAD):
         z_start(n)
     stage_b(2)
     acts = {"B": stage_b, "C": stage_c, "D": stage_d, "F": finish_hidden, "R": relay_hidden, "L": last_hidden}
     for step in PLAN:
         act, n = step[0], int(step[1:])
-        if act == "P":
-            p_copy(n).start()
-        elif act == "H":
+        if act == "H":
             for m in range(4):
                 hess_part(n, m)
         elif act == "E":
@@ -479,8 +483,9 @@
     for i in range(len(PIECES)):
         for n in range(4):
             x_copy(i, n).wait_send()
+    for j in range(NZ):
+        p_copy(j).wait_send()
     for g in range(len(GROUPS)):
-        p_copy(g).wait_send()
         for n in range(4):
             hx_copy(g, n).wait_send()
             hc_copy(g, n).wait_send()
@@ -541,8 +546,8 @@
             sem((len(PIECES), 4)),
             sem((2, 2)),
             sem((4,)),
-            sem((groups,)),
-            sem((groups,)),
+            sem((NZ,)),
+            sem((NZ,)),
             sem((groups, 4)),
             sem((groups, 4)),
             sem((groups, 4)),

time: 112 us -> 112 us (level)
  no operation moved by 1% of the time
where the time goes in v4:
time: 112 us
  Pallas kernels  108 us (96%)
  local copies, waits for them, and re-layouts  3.55 us (3%)
    pallas_call x1, Pallas kernels, shards(): pl.pallas_call(functools.partial(kernel, scale_out), out_shape=(jax.Shape...  108 us
    unnamed x2, local copies, waits for them, and re-layouts  3.55 us

profile of v4, /device:TPU:1, one launch (start us, length us, event | category | flops | bytes accessed | tf_op | source)
XLA Modules:
  0.0 111.9 jit_solution(13981482382705411945)
XLA Ops:
  0.6 107.7 %routed_stats.1 = (bf16[1024,128]{1,0:T(8,128)(2,1)}, f32[128,1024]{1,0:T(8,128)}) custom-call(bf16[8,7168]{1,0:T(8,128)(2,1)} %codes_in.1, s32[8,56]{1,0:T(8,128)} %exponents_in.1, s32[8,8]{1,0:T(8,128)} %routes_in.1, bf16[7168,128]{1,0:T(8,128)(2,1)} %bitcast.4, bf16[7168,128]{1,0:T(8,128)(2,1)} %bitcast.5), custom_call_target="tpu_custom_call" | custom-call | tf_op jit(solution)/shard_map/routed_stats/pallas_call | solution.py:511
  108.4 1.7 %copy.9 = bf16[1,1024,128]{2,1,0:T(8,128)(2,1)} copy(bf16[1,1024,128]{2,1,0:T(8,128)(2,1)} %bitcast.7) | data formatting | bytes 524288
  110.0 1.9 %copy.10 = f32[1,128,1024]{2,1,0:T(8,128)} copy(f32[1,128,1024]{2,1,0:T(8,128)} %bitcast.6) | data formatting | bytes 1048576
